TPU v7x, 32 devices: a whole 2x2x4 slice. The times are simulated.
32 devices in a mesh: seq: 16 (over z, y, x), mlp: 2 (over core).
Axes of the slice: x: 2, y: 2, z: 4, core: 2. Of those that a mesh axis runs over, the one named last changes fastest.
Arguments:
- queries: bfloat16 [4096, 3072], P('seq', 'mlp'), may hold values from -5 to 5
- key_vectors: bfloat16 [4096, 3072], P('seq', 'mlp'), may hold values from -5 to 5
- value_vectors: bfloat16 [4096, 3072], P('seq', 'mlp'), may hold values from -6 to 6
- head_kinds: int32 [24], P('mlp'), may hold values from 0 to 1
- block_masks: int32 [24, 2, 2], P('mlp'), may hold values from 0 to 1, as said below
- order_map: int32 [256], replicated, may hold values from 0 to 255, as said below
- out_weight: bfloat16 [3072, 3072], P('seq', 'mlp'), may hold values from -0.109375 to 0.109375
- gate_values: float32 [3072], P('mlp'), may hold values from 0.5 to 2
Outputs:
- gated_output: bfloat16 [4096, 3072], P('seq', 'mlp')
Inputs may be any that keep to these rules, and one draw needn't show every extreme that they name: block_masks[h, b, b] = 1 for every head h and block b. A permutation of the 256 positions in which order_map[2 i] is even and order_map[2 i + 1] = order_map[2 i] + 1.
All inputs are finite; a program needn't handle non-finite values.
Results may differ from a plain program's by a relative error of at most 0.0056.
Values may be sent and summed in bfloat16 or wider, within the bound.
A program may use at most 64 MiB of HBM per device.

v0:
```python
import math

import jax
import jax.numpy as jnp
from jax import lax
from jax.sharding import PartitionSpec as P


def attend_rows(query_rows, key_rows, value_rows, visible):
    row_count, head_count, head_depth = query_rows.shape
    score_scale = 1.0 / math.sqrt(head_depth)
    scores = (
        jnp.einsum("qhd,khd->hqk", query_rows, key_rows, preferred_element_type=jnp.float32)
        * score_scale
    )
    row_max = jnp.max(jnp.where(visible, scores, -jnp.inf), axis=2, keepdims=True)
    weights = jnp.where(visible, jnp.exp(scores - row_max), 0.0)
    row_total = jnp.sum(weights, axis=2)
    combined = jnp.einsum(
        "hqk,khd->qhd", weights.astype(jnp.bfloat16), value_rows, preferred_element_type=jnp.float32
    )
    outputs = (combined / jnp.transpose(row_total)[:, :, None]).astype(jnp.bfloat16)
    return outputs


def to_positions(query_rows, key_rows, value_rows, frames, group_size):
    row_width = query_rows.shape[1]
    exchanged = (
        lax.all_to_all(
            query_rows.reshape(frames, group_size, 1, row_width),
            "seq",
            split_axis=0,
            concat_axis=2,
            tiled=True,
        ),
        lax.all_to_all(
            key_rows.reshape(frames, group_size, 1, row_width),
            "seq",
            split_axis=0,
            concat_axis=2,
            tiled=True,
        ),
        lax.all_to_all(
            value_rows.reshape(frames, group_size, 1, row_width),
            "seq",
            split_axis=0,
            concat_axis=2,
            tiled=True,
        ),
    )
    return tuple((member.reshape(group_size * frames, row_width) for member in exchanged))


def to_frames(results, frames, group_size):
    row_width = results.shape[1]
    exchanged = lax.all_to_all(
        results.reshape(1, group_size, frames, row_width),
        "seq",
        split_axis=2,
        concat_axis=0,
        tiled=True,
    )
    return exchanged.reshape(frames * group_size, row_width)


def split_heads(array, head_count):
    return array.reshape(array.shape[0], head_count, array.shape[1] // head_count)


def local(
    queries, key_vectors, value_vectors, head_kinds, block_masks, order_map, out_weight, gate_values
):
    row_count, row_width = queries.shape
    head_count = head_kinds.shape[0]
    frames = lax.axis_size("seq")
    group_size = row_count // frames
    block_size = row_count // block_masks.shape[1]
    inverse = (
        jnp.zeros((row_count,), jnp.int32).at[order_map].set(jnp.arange(row_count, dtype=jnp.int32))
    )
    visible = jnp.repeat(jnp.repeat(block_masks == 1, block_size, axis=1), block_size, axis=2)
    temporal = (head_kinds == 1)[None, :, None]
    moved_queries, moved_keys, moved_values = to_positions(
        queries[order_map], key_vectors[order_map], value_vectors[order_map], frames, group_size
    )
    near_result = attend_rows(
        split_heads(queries, head_count),
        split_heads(key_vectors, head_count),
        split_heads(value_vectors, head_count),
        visible,
    )
    far_result = attend_rows(
        split_heads(moved_queries, head_count),
        split_heads(moved_keys, head_count),
        split_heads(moved_values, head_count),
        visible,
    )
    returned = to_frames(far_result.reshape(row_count, row_width), frames, group_size)[inverse]
    per_head = jnp.where(temporal, split_heads(returned, head_count), near_result)
    attended = per_head.reshape(row_count, row_width)
    head_columns = lax.all_gather(attended, "mlp", axis=1, tiled=True)
    projected = jnp.dot(
        head_columns,
        lax.all_gather(out_weight, "seq", axis=0, tiled=True),
        preferred_element_type=jnp.float32,
    )
    return (gate_values[None, :] * projected).astype(jnp.bfloat16)


def solution(mesh):
    in_specs = (
        P("seq", "mlp"),
        P("seq", "mlp"),
        P("seq", "mlp"),
        P("mlp"),
        P("mlp", None, None),
        P(),
        P("seq", "mlp"),
        P("mlp"),
    )
    out_specs = P("seq", "mlp")
    return jax.shard_map(local, mesh=mesh, in_specs=in_specs, out_specs=out_specs, check_vma=False)
```

profile of v0, /device:TPU:0, one launch (start us, length us, event | category | flops | bytes accessed | tf_op | source)
XLA Modules:
  0.0 273.9 jit_solution(5623304353242160316)
XLA Ops:
  6.5 0.7 compare_select_fusion.1
  7.2 4.2 %gather_fusion.1 = bf16[256,1536]{1,0:T(8,128)(2,1)} fusion(bf16[256,1536]{1,0:T(8,128)(2,1)} %param.8, s32[1024]{0:T(1024)S(1)} %pad_clamp_fusion.1), kind=kCustom, calls=%fused_computation.1 | custom fusion | bytes 1573888 | tf_op jit(solution)/shard_map/gather | solution.py:84
  11.4 8.3 %all-to-all-start.1 = ((bf16[16,16,1,1536]{3,1,2,0:T(8,128)(2,1)}), bf16[16,16,1,1536]{3,1,2,0:T(8,128)(2,1)S(1)}, u32[]{:S(2)}, u32[]{:S(2)}) async-start(bf16[16,16,1,1536]{3,1,2,0:T(8,128)(2,1)} %bitcast.6), calls=%async_computation.1 | async-start | bytes 1572864 | tf_op jit(solution)/shard_map/all_to_all | solution.py:29
  19.8 2.1 gather_fusion.2
  21.9 17.6 %all-to-all-done.1 = bf16[16,16,1,1536]{3,1,2,0:T(8,128)(2,1)S(1)} async-done(((bf16[16,16,1,1536]{3,1,2,0:T(8,128)(2,1)}), bf16[16,16,1,1536]{3,1,2,0:T(8,128)(2,1)S(1)}, u32[]{:S(2)}, u32[]{:S(2)}) %all-to-all-start.1) | async-done | bytes 786464 | tf_op jit(solution)/shard_map/all_to_all | solution.py:29
  39.5 4.9 %all-to-all-start.2 = ((bf16[16,16,1,1536]{3,1,2,0:T(8,128)(2,1)}), bf16[16,16,1,1536]{3,1,2,0:T(8,128)(2,1)}, u32[]{:S(2)}, u32[]{:S(2)}) async-start(bf16[16,16,1,1536]{3,1,2,0:T(8,128)(2,1)} %bitcast.10), calls=%async_computation.2 | async-start | bytes 1572864 | tf_op jit(solution)/shard_map/all_to_all | solution.py:36
  44.5 2.1 gather_fusion
  46.6 16.5 %all-to-all-done.2 = bf16[16,16,1,1536]{3,1,2,0:T(8,128)(2,1)} async-done(((bf16[16,16,1,1536]{3,1,2,0:T(8,128)(2,1)}), bf16[16,16,1,1536]{3,1,2,0:T(8,128)(2,1)}, u32[]{:S(2)}, u32[]{:S(2)}) %all-to-all-start.2) | async-done | bytes 786464 | tf_op jit(solution)/shard_map/all_to_all | solution.py:36
  63.1 4.9 %all-to-all-start = ((bf16[16,16,1,1536]{3,1,2,0:T(8,128)(2,1)}), bf16[16,16,1,1536]{3,1,2,0:T(8,128)(2,1)}, u32[]{:S(2)}, u32[]{:S(2)}) async-start(bf16[16,16,1,1536]{3,1,2,0:T(8,128)(2,1)} %bitcast.72), calls=%async_computation | async-start | bytes 1572864 | tf_op jit(solution)/shard_map/all_to_all | solution.py:43
  68.1 1.2 copy.51
  69.3 1.1 copy.52
  71.7 2.4 copy.43
  74.2 1.6 reshape_reshape.14
  77.2 3.5 %bitcast_select_fusion.1 = (f32[12,256,256]{1,2,0:T(8,128)}, f32[12,256,256]{1,2,0:T(8,128)S(1)}, f32[12,256,256]{1,2,0:T(8,128)}) fusion(pred[12,256,2]{1,2,0:T(4,128)(4,1)S(1)} %copy.39, f32[12,256,256]{1,2,0:T(8,128)S(1)} %fusion.17, bf16[256,12,128]{0,2,1:T(8,128)(2,1)S(1)} %bitcast.69, bf16[256,12,128]{0,2,1:T(8,128)(2,1)S(1)} %bitcast.70), kind=kOutput, calls=%fused_computation.8 | convolution fusion | flops 204472320 | bytes 14161920 | tf_op jit(solution)/shard_map/qhd,khd->hqk/dot_general | solution.py:13
  80.7 0.9 fusion.22
  81.6 5.2 %all-to-all-done = bf16[16,16,1,1536]{3,1,2,0:T(8,128)(2,1)} async-done(((bf16[16,16,1,1536]{3,1,2,0:T(8,128)(2,1)}), bf16[16,16,1,1536]{3,1,2,0:T(8,128)(2,1)}, u32[]{:S(2)}, u32[]{:S(2)}) %all-to-all-start) | async-done | bytes 786464 | tf_op jit(solution)/shard_map/all_to_all | solution.py:43
  86.8 1.6 copy.37
  88.3 1.5 reshape_reshape.12
  89.9 2.6 fusion.4
  92.4 1.9 copy.48
  94.9 1.3 copy.49
  96.2 4.9 %all-to-all-start.3 = ((bf16[1,16,16,1536]{3,1,0,2:T(8,128)(2,1)}), bf16[1,16,16,1536]{3,1,0,2:T(8,128)(2,1)S(1)}, u32[]{:S(2)}, u32[]{:S(2)}) async-start(bf16[1,16,16,1536]{3,1,0,2:T(8,128)(2,1)} %copy.49), calls=%async_computation.3 | async-start | bytes 1572864 | tf_op jit(solution)/shard_map/all_to_all | solution.py:56
  101.1 1.2 copy.55
  102.3 1.4 scatter_custom_fusion
  103.8 3.7 %fusion.23 = (f32[12,256]{1,0:T(8,128)S(1)}, bf16[12,256,256]{1,2,0:T(8,128)(2,1)S(1)}) fusion(f32[12,256,256]{1,2,0:T(8,128)} %get-tuple-element.5, f32[12,256,256]{1,2,0:T(8,128)} %get-tuple-element.7, pred[12,256,2]{1,2,0:T(4,128)(4,1)S(1)} %copy.39), kind=kOutput, calls=%fused_computation.35 | output fusion | flops 3932415 | bytes 7882752 | tf_op jit(solution)/shard_map/sub | solution.py:17
  107.5 12.2 %all-to-all-done.3 = bf16[1,16,16,1536]{3,1,0,2:T(8,128)(2,1)S(1)} async-done(((bf16[1,16,16,1536]{3,1,0,2:T(8,128)(2,1)}), bf16[1,16,16,1536]{3,1,0,2:T(8,128)(2,1)S(1)}, u32[]{:S(2)}, u32[]{:S(2)}) %all-to-all-start.3) | async-done | bytes 786464 | tf_op jit(solution)/shard_map/all_to_all | solution.py:56
  119.7 1.3 gather_fusion.3
  121.2 2.4 fusion.13
  123.7 0.7 all-gather.5.cloned.1.call-update
  124.4 8.5 %all-gather.3.cloned.1.call-done = bf16[256,3072]{0,1:T(8,128)(2,1)} async-done(((bf16[256,1536]{0,1:T(8,128)(2,1)}), bf16[256,3072]{0,1:T(8,128)(2,1)}) %all-gather.3.cloned.1.call-update) | async-done | bytes 1572880 | tf_op jit(solution)/shard_map/all_gather | solution.py:101
  132.9 126.5 %all-gather.5.cloned.1.call-done = bf16[3072,1536]{1,0:T(8,128)(2,1)} async-done(((bf16[192,1536]{1,0:T(8,128)(2,1)}), bf16[3072,1536]{1,0:T(8,128)(2,1)}) %all-gather.5.cloned.1.call-update) | async-done | bytes 9437200 | tf_op jit(solution)/shard_map/all_gather | solution.py:104
  259.4 7.7 %fusion.2 = bf16[256,1536]{1,0:T(8,128)(2,1)} fusion(bf16[256,3072]{0,1:T(8,128)(2,1)} %all-gather.3.cloned.1.call-done, bf16[3072,1536]{1,0:T(8,128)(2,1)} %all-gather.5.cloned.1.call-done, f32[1536]{0:T(1024)S(1)} %copy-done.5), kind=kOutput, calls=%fused_computation.12 | convolution fusion | flops 2416705536 | bytes 11802624 | tf_op jit(solution)/shard_map/dot_general | solution.py:102
  (34 shorter events, 3.5 us)
Async XLA Ops:
  7.2 12.5 %copy-start.1 = (bf16[256,1536]{1,0:T(8,128)(2,1)S(1)}, bf16[256,1536]{1,0:T(8,128)(2,1)}, u32[]{:S(2)}) copy-start(bf16[256,1536]{1,0:T(8,128)(2,1)} %param.9) | copy-start | bytes 2359300
  11.4 28.1 %all-to-all-start.1 = ((bf16[16,16,1,1536]{3,1,2,0:T(8,128)(2,1)}), bf16[16,16,1,1536]{3,1,2,0:T(8,128)(2,1)S(1)}, u32[]{:S(2)}, u32[]{:S(2)}) async-start(bf16[16,16,1,1536]{3,1,2,0:T(8,128)(2,1)} %bitcast.6), calls=%async_computation.1 | async-start | bytes 1572864 | tf_op jit(solution)/shard_map/all_to_all | solution.py:29
  19.8 24.7 %copy-start.2 = (bf16[256,1536]{1,0:T(8,128)(2,1)S(1)}, bf16[256,1536]{1,0:T(8,128)(2,1)}, u32[]{:S(2)}) copy-start(bf16[256,1536]{1,0:T(8,128)(2,1)} %param.10) | copy-start | bytes 2359300
  39.5 23.7 %all-to-all-start.2 = ((bf16[16,16,1,1536]{3,1,2,0:T(8,128)(2,1)}), bf16[16,16,1,1536]{3,1,2,0:T(8,128)(2,1)}, u32[]{:S(2)}, u32[]{:S(2)}) async-start(bf16[16,16,1,1536]{3,1,2,0:T(8,128)(2,1)} %bitcast.10), calls=%async_computation.2 | async-start | bytes 1572864 | tf_op jit(solution)/shard_map/all_to_all | solution.py:36
  44.5 23.6 %copy-start = (bf16[256,1536]{1,0:T(8,128)(2,1)S(1)}, bf16[256,1536]{1,0:T(8,128)(2,1)}, u32[]{:S(2)}) copy-start(bf16[256,1536]{1,0:T(8,128)(2,1)} %param.8) | copy-start | bytes 2359300
  46.6 23.8 %copy-start.6 = (s32[12,2,2]{0,2,1:T(2,128)S(1)}, s32[12,2,2]{0,2,1:T(2,128)}, u32[]{:S(2)}) copy-start(s32[12,2,2]{0,2,1:T(2,128)} %param.12) | copy-start | bytes 580
  63.1 23.6 %all-to-all-start = ((bf16[16,16,1,1536]{3,1,2,0:T(8,128)(2,1)}), bf16[16,16,1,1536]{3,1,2,0:T(8,128)(2,1)}, u32[]{:S(2)}, u32[]{:S(2)}) async-start(bf16[16,16,1,1536]{3,1,2,0:T(8,128)(2,1)} %bitcast.72), calls=%async_computation | async-start | bytes 1572864 | tf_op jit(solution)/shard_map/all_to_all | solution.py:43
  75.8 1.1 copy-start.3
  75.8 1.4 copy-start.4
  94.3 9.4 %copy-start.7 = (s32[12]{0:T(128)S(1)}, s32[12]{0:T(128)}, u32[]{:S(2)}) copy-start(s32[12]{0:T(128)} %param.11) | copy-start | bytes 148
  96.2 23.5 %all-to-all-start.3 = ((bf16[1,16,16,1536]{3,1,0,2:T(8,128)(2,1)}), bf16[1,16,16,1536]{3,1,0,2:T(8,128)(2,1)S(1)}, u32[]{:S(2)}, u32[]{:S(2)}) async-start(bf16[1,16,16,1536]{3,1,0,2:T(8,128)(2,1)} %copy.49), calls=%async_computation.3 | async-start | bytes 1572864 | tf_op jit(solution)/shard_map/all_to_all | solution.py:56
  101.1 31.8 %all-gather.3.cloned.1.call-start = ((), (), s32[]{:S(2)}) async-start(), calls=%async_computation.4 | async-start | bytes 2359296 | tf_op jit(solution)/shard_map/all_gather | solution.py:101
  121.2 138.1 %copy-start.5 = (f32[1536]{0:T(1024)S(1)}, f32[1536]{0:T(1024)}, u32[]{:S(2)}) copy-start(f32[1536]{0:T(1024)} %param.15) | copy-start | bytes 18436
  123.7 135.7 %all-gather.5.cloned.1.call-start = ((), (), s32[]{:S(2)}) async-start(), calls=%async_computation.5 | async-start | bytes 10027008 | tf_op jit(solution)/shard_map/all_gather | solution.py:104
Sparse Core Ops, SparseCore 0:
  123.8 9.0 all-gather.2
  135.7 123.6 all-gather.4
where the time goes:
time: 275 us; the launch traced here: 274 us
  waiting for transfers between devices  187 us (68%)
  local copies, waits for them, and re-layouts  27.8 us (10%)
  starting transfers between devices  23.2 us (8%)
  matrix products  16.8 us (6%)
  between operations  13.6 us (5%)
  other arithmetic  5.31 us (2%)
    all_gather x1, waiting for transfers between devices, local(): lax.all_gather(out_weight, 'seq', axis=0, tiled=True)  126 us
    all_to_all x1, waiting for transfers between devices, to_positions(): lax.all_to_all(query_rows.reshape(frames, group_size, 1, row_width), 'seq...  17.6 us
    all_to_all x1, waiting for transfers between devices, to_positions(): lax.all_to_all(key_rows.reshape(frames, group_size, 1, row_width), 'seq',...  16.5 us
    all_to_all x1, waiting for transfers between devices, to_frames(): lax.all_to_all(results.reshape(1, group_size, frames, row_width), 'seq',...  12.2 us
    all_gather x1, waiting for transfers between devices, local(): head_columns = lax.all_gather(attended, 'mlp', axis=1, tiled=True)  8.48 us
    all_to_all x1, starting transfers between devices, to_positions(): lax.all_to_all(query_rows.reshape(frames, group_size, 1, row_width), 'seq...  8.31 us
    dot_general x1, matrix products, local(): jnp.dot(head_columns, lax.all_gather(out_weight, 'seq', axis=0, tiled=Tru...  7.66 us
  transfers between devices with their start and end apart: 6, of which 6 were waited for; matrix products, arithmetic and copies ran while one was open for 8% of the time, Pallas kernels for 0%

commit v1 on v0

--- a/solution.py
+++ b/solution.py
@@ -1,8 +1,11 @@
+import functools
 import math
 
 import jax
 import jax.numpy as jnp
 from jax import lax
+from jax.experimental import pallas as pl
+from jax.experimental.pallas import tpu as pltpu
 from jax.sharding import PartitionSpec as P
 
 
@@ -107,6 +110,342 @@
     return (gate_values[None, :] * projected).astype(jnp.bfloat16)
 
 
+PLANE = 4
+MESH = pl.DeviceIdType.MESH
+
+
+def aligned(index, size):
+    return pl.ds(pl.multiple_of(index * size, size), size)
+
+
+def branch_kernel(
+    frames, slots, depth,
+    heads_ref, kinds_ref, bias_ref, order_ref, q_ref, k_ref, v_ref, w_ref, gate_ref,
+    out_ref,
+    packed, moved, result, returned, attended, w_rows, w_slots, part_out, part_own, part_in,
+    done_out, done,
+    qkv_send, qkv_recv, res_send, res_recv, near_send, near_recv, far_send, far_recv,
+    w1_send, w1_recv, w1_own, w2_send, w2_recv, p_send, p_recv, o_send, o_recv,
+):
+    rows, width = q_ref.shape
+    heads = width // depth
+    group = rows // frames
+    layers = frames // PLANE
+    half_layers = layers // 2
+    w_part, columns = w_ref.shape[0], width // PLANE
+    me, m = lax.axis_index("seq"), lax.axis_index("mlp")
+    z, p = me // PLANE, me % PLANE
+    scale = 1.0 / math.sqrt(depth)
+    bf16, f32 = jnp.bfloat16, jnp.float32
+
+    def remote(src, dst, send, recv, seq, mlp):
+        return pltpu.make_async_remote_copy(
+            src_ref=src, dst_ref=dst, send_sem=send, recv_sem=recv,
+            device_id=(seq, mlp), device_id_type=MESH,
+        )
+
+    barrier = pltpu.get_barrier_semaphore()
+    for d in range(frames):
+        peer = (me + d) % frames
+        if d:
+            pl.semaphore_signal(barrier, inc=1, device_id=(peer, m), device_id_type=MESH)
+        pl.semaphore_signal(barrier, inc=1, device_id=(peer, 1 - m), device_id_type=MESH)
+
+    places = lax.broadcasted_iota(jnp.int32, (rows, rows), 0)
+    back_f32 = jnp.where(places == order_ref[...], 1.0, 0.0)
+    back = back_f32.astype(bf16)
+    forth = back_f32.T.astype(bf16)
+
+    def head_of(t):
+        return t if slots == heads else heads_ref[t]
+
+    def pack(t, carry):
+        h = head_of(t)
+        for i, ref in enumerate((q_ref, k_ref, v_ref)):
+            block = jnp.dot(forth, ref[:, aligned(h, depth)], preferred_element_type=f32)
+            packed[:, :, aligned(3 * t + i, depth)] = block.astype(bf16).reshape(frames, group, depth)
+        return carry
+
+    lax.fori_loop(0, slots, pack, 0)
+    pl.semaphore_wait(barrier, 2 * frames - 1)
+
+    def qkv_copy(d, to, slot):
+        return remote(packed.at[to], moved.at[slot], qkv_send.at[d], qkv_recv.at[d], to, m)
+
+    for d in range(1, frames):
+        qkv_copy(d, (me + d) % frames, me).start()
+    moved[me] = packed[me]
+
+    core = z // half_layers
+    layer = z % half_layers
+
+    def w1_copy(d, to, source, source_m):
+        return remote(
+            w_ref.at[:, aligned(to, columns)],
+            w_rows.at[source_m, aligned(layer * PLANE + source, w_part), :],
+            w1_send.at[d], w1_recv.at[d, source_m], z * PLANE + to, core,
+        )
+
+    for d in range(1, PLANE):
+        w1_copy(d, (p + d) % PLANE, p, m).start()
+
+    @pl.when(m != core)
+    def _():
+        w1_copy(0, p, p, m).start()
+
+    own_copy = pltpu.make_async_copy(
+        w_ref.at[:, aligned(p, columns)],
+        w_rows.at[m, aligned(layer * PLANE + p, w_part), :],
+        w1_own,
+    )
+
+    @pl.when(m == core)
+    def _():
+        own_copy.start()
+
+    row_ids = lax.broadcasted_iota(jnp.int32, (rows, rows), 0)
+    col_ids = lax.broadcasted_iota(jnp.int32, (rows, rows), 1)
+    block = rows // 2
+    part = block // frames
+    assert 2 * block == rows and 2 * part == group
+
+    def attend(q, k, v, t, row_block, col_block):
+        levels = bias_ref[t]
+        levels = jnp.concatenate([levels, levels], axis=1)
+        first = col_block[0:1] == 0
+        upper = jnp.where(first, levels[0:1], levels[1:2])
+        lower = jnp.where(first, levels[2:3], levels[3:4])
+        bias = jnp.where(row_block == 0, upper, lower)
+        scores = lax.dot_general(q, k, (((1,), (1,)), ((), ())), preferred_element_type=f32)
+        scores = scores * scale + bias
+        weights = jnp.exp(scores - jnp.max(scores, axis=1, keepdims=True))
+        total = jnp.sum(weights, axis=1, keepdims=True)
+        mixed = jnp.dot(weights.astype(bf16), v, preferred_element_type=f32)
+        return (mixed / total).astype(bf16)
+
+    def near_head(t, carry):
+        at = aligned(head_of(t), depth)
+        attended[p, :, aligned(t, depth)] = attend(
+            q_ref[:, at], k_ref[:, at], v_ref[:, at], t, row_ids // block, col_ids // block
+        )
+        return carry
+
+    far_cols, near_cols = pl.ds(0, slots * depth), pl.ds(slots * depth, (heads - slots) * depth)
+
+    def near_copy(d, to, source):
+        ref = attended.at[source, :, near_cols]
+        return remote(ref, ref, near_send.at[d], near_recv.at[d], z * PLANE + to, m)
+
+    def far_copy(d, to, source):
+        ref = attended.at[source, :, far_cols]
+        return remote(ref, ref, far_send.at[d], far_recv.at[d], z * PLANE + to, m)
+
+    if slots < heads:
+        lax.fori_loop(slots, heads, near_head, 0)
+        for d in range(1, PLANE):
+            near_copy(d, (p + d) % PLANE, p).start()
+    lax.fori_loop(0, slots, near_head, 0)
+
+    @pl.when(m != core)
+    def _():
+        w1_copy(0, p, p, m).wait_send()
+
+    @pl.when(m == core)
+    def _():
+        own_copy.wait()
+        for d in range(PLANE):
+            source = (p + PLANE - d) % PLANE
+            if d:
+                w1_copy(d, p, source, m).wait_recv()
+            w1_copy(d, p, source, 1 - m).wait_recv()
+
+    for d in range(1, PLANE):
+        w1_copy(d, (p + d) % PLANE, p, m).wait_send()
+
+    def line_copy(b, way, to):
+        ref = w_rows.at[:, pl.ds(b * PLANE * w_part, PLANE * w_part), :]
+        return remote(ref, ref, w2_send.at[b, way], w2_recv.at[b], to * PLANE + p, m)
+
+    def line_round(step):
+        for b in range(half_layers):
+            distance = z - (m * half_layers + b)
+            if step:
+                @pl.when(jnp.logical_or(distance == step, distance == -step))
+                def _():
+                    line_copy(b, 0, z).wait_recv()
+
+            @pl.when(jnp.logical_and(distance == step, z < layers - 1))
+            def _():
+                line_copy(b, 0, z + 1).start()
+
+            @pl.when(jnp.logical_and(distance == -step, z > 0))
+            def _():
+                line_copy(b, 1, z - 1).start()
+
+    def line_end():
+        for b in range(half_layers):
+            distance = z - (m * half_layers + b)
+
+            @pl.when(jnp.logical_and(distance >= 0, z < layers - 1))
+            def _():
+                line_copy(b, 0, z).wait_send()
+
+            @pl.when(jnp.logical_and(distance <= 0, z > 0))
+            def _():
+                line_copy(b, 1, z).wait_send()
+
+    for d in range(1, frames):
+        qkv_copy(d, me, (me + frames - d) % frames).wait_recv()
+    line_round(0)
+
+    def far_head(t, carry):
+        q, k, v = (moved[:, :, aligned(3 * t + i, depth)].reshape(rows, depth) for i in range(3))
+        mixed = attend(q, k, v, t, (row_ids % group) // part, (col_ids % group) // part)
+        result[:, :, aligned(t, depth)] = mixed.reshape(frames, group, depth)
+        return carry
+
+    lax.fori_loop(0, slots, far_head, 0)
+
+    def res_copy(d, to, slot):
+        return remote(result.at[to], returned.at[slot], res_send.at[d], res_recv.at[d], to, m)
+
+    for d in range(1, frames):
+        res_copy(d, (me + d) % frames, me).start()
+    returned[me] = result[me]
+    line_round(1)
+    for d in range(1, frames):
+        res_copy(d, me, (me + frames - d) % frames).wait_recv()
+
+    def unpack(t, carry):
+        at = aligned(t, depth)
+        rows_back = jnp.dot(back, returned[:, :, at].reshape(rows, depth), preferred_element_type=f32)
+        temporal = kinds_ref[:, at] == 1
+        attended[p, :, at] = jnp.where(temporal, rows_back, attended[p, :, at].astype(f32)).astype(bf16)
+        return carry
+
+    lax.fori_loop(0, slots, unpack, 0)
+    for d in range(1, PLANE):
+        far_copy(d, (p + d) % PLANE, p).start()
+    for step in range(2, layers):
+        line_round(step)
+    line_end()
+
+    def order_rows(t, carry):
+        at = aligned(t, depth)
+        source = aligned(head_of(t), depth)
+        w_slots[0, at, :] = w_rows[0, source, :]
+        w_slots[1, at, :] = w_rows[1, source, :]
+        return carry
+
+    lax.fori_loop(0, heads, order_rows, 0)
+
+    def part_copy(d):
+        return remote(part_out.at[d], part_in.at[d], p_send.at[d], p_recv.at[d], me, 1 - m)
+
+    for d in range(PLANE):
+        source = (p + PLANE - d) % PLANE
+        if d:
+            if slots < heads:
+                near_copy(d, p, source).wait_recv()
+            far_copy(d, p, source).wait_recv()
+        rows_in = attended[source]
+        part_out[d] = jnp.dot(rows_in, w_slots[1 - m], preferred_element_type=f32)
+        part_copy(d).start()
+        part_own[d] = jnp.dot(rows_in, w_slots[m], preferred_element_type=f32)
+
+    gate = gate_ref[:, aligned(p, columns)]
+
+    def done_copy(d, to, source):
+        return remote(
+            done_out.at[d], done.at[:, aligned(source, columns)],
+            o_send.at[d], o_recv.at[d], z * PLANE + to, m,
+        )
+
+    for d in range(PLANE):
+        part_copy(d).wait_recv()
+        gated = (gate * (part_own[d] + part_in[d])).astype(bf16)
+        if d:
+            done_out[d] = gated
+            done_copy(d, (p + PLANE - d) % PLANE, p).start()
+        else:
+            done[:, aligned(p, columns)] = gated
+    for d in range(1, frames):
+        qkv_copy(d, (me + d) % frames, me).wait_send()
+        res_copy(d, (me + d) % frames, me).wait_send()
+    for d in range(PLANE):
+        part_copy(d).wait_send()
+    for d in range(1, PLANE):
+        if slots < heads:
+            near_copy(d, (p + d) % PLANE, p).wait_send()
+        far_copy(d, (p + d) % PLANE, p).wait_send()
+        done_copy(d, (p + PLANE - d) % PLANE, p).wait_send()
+        done_copy(d, p, (p + d) % PLANE).wait_recv()
+    out_ref[...] = done[...]
+
+
+def branch_call(frames, slots, head_order, slot_kinds, slot_bias, order_map, q, k, v, w, gate):
+    rows, width = q.shape
+    heads = slot_bias.shape[0]
+    depth = width // heads
+    group, columns = rows // frames, width // PLANE
+    half = w.shape[0] * frames // 2
+    half_layers = frames // PLANE // 2
+    bf16, f32, dma = jnp.bfloat16, jnp.float32, pltpu.SemaphoreType.DMA
+    smem, vmem = pl.BlockSpec(memory_space=pltpu.SMEM), pl.BlockSpec(memory_space=pltpu.VMEM)
+    return pl.pallas_call(
+        functools.partial(branch_kernel, frames, slots, depth),
+        out_shape=jax.ShapeDtypeStruct((rows, width), bf16),
+        in_specs=[smem] + [vmem] * 8,
+        out_specs=vmem,
+        scratch_shapes=[
+            pltpu.VMEM((frames, group, 3 * slots * depth), bf16),
+            pltpu.VMEM((frames, group, 3 * slots * depth), bf16),
+            pltpu.VMEM((frames, group, slots * depth), bf16),
+            pltpu.VMEM((frames, group, slots * depth), bf16),
+            pltpu.VMEM((PLANE, rows, width), bf16),
+            pltpu.VMEM((2, half, columns), bf16),
+            pltpu.VMEM((2, half, columns), bf16),
+            pltpu.VMEM((PLANE, rows, columns), f32),
+            pltpu.VMEM((PLANE, rows, columns), f32),
+            pltpu.VMEM((PLANE, rows, columns), f32),
+            pltpu.VMEM((PLANE, rows, columns), bf16),
+            pltpu.VMEM((rows, width), bf16),
+            dma((frames,)), dma((frames,)), dma((frames,)), dma((frames,)),
+            dma((PLANE,)), dma((PLANE,)), dma((PLANE,)), dma((PLANE,)),
+            dma((PLANE,)), dma((PLANE, 2)), dma(()), dma((half_layers, 2)), dma((half_layers,)),
+            dma((PLANE,)), dma((PLANE,)), dma((PLANE,)), dma((PLANE,)),
+        ],
+        compiler_params=pltpu.CompilerParams(
+            collective_id=slots, has_side_effects=True, vmem_limit_bytes=48 * 2**20
+        ),
+        name="branch_%d" % slots,
+    )(
+        head_order, slot_kinds, slot_bias, order_map.reshape(1, rows),
+        q, k, v, w, gate.reshape(1, width),
+    )
+
+
+def fused_local(q, k, v, head_kinds, block_masks, order_map, out_weight, gate_values):
+    frames = lax.axis_size("seq")
+    heads = head_kinds.shape[0]
+    depth = q.shape[1] // heads
+    bias = jnp.where(block_masks == 1, 0.0, -1e30).reshape(heads, 4)
+
+    def call(slots, order, kinds, bias):
+        return branch_call(
+            frames, slots, order, jnp.repeat(kinds, depth)[None, :],
+            jnp.broadcast_to(bias[:, :, None], (heads, 4, depth)),
+            order_map, q, k, v, out_weight, gate_values,
+        )
+
+    return call(heads, jnp.arange(heads, dtype=jnp.int32), head_kinds, bias)
+
+
+def fits(mesh):
+    frames = mesh.shape["seq"]
+    return mesh.shape["mlp"] == 2 and frames % (2 * PLANE) == 0 and frames <= 16
+
+
 def solution(mesh):
     in_specs = (
         P("seq", "mlp"),
@@ -119,4 +458,5 @@
         P("mlp"),
     )
     out_specs = P("seq", "mlp")
-    return jax.shard_map(local, mesh=mesh, in_specs=in_specs, out_specs=out_specs, check_vma=False)
+    body = fused_local if fits(mesh) else local
+    return jax.shard_map(body, mesh=mesh, in_specs=in_specs, out_specs=out_specs, check_vma=False)

time: 275 us -> 151 us (0.55)
  waiting for transfers between devices: 187 us -> 0 us
  Pallas kernels: 0 us -> 143 us
  starting transfers between devices: 23.2 us -> 0 us
  local copies, waits for them, and re-layouts: 27.8 us -> 7.49 us
  matrix products: 16.8 us -> 0 us
  between operations: 13.6 us -> 0.03 us
  other arithmetic: 5.31 us -> 0.01 us
    pallas_call x0 -> x1, Pallas kernels: none -> 143 us  [branch_call(): pl.pallas_call(functools.partial(branch_kernel, frames, slots, depth), ou...]
    all_gather x2 -> x0, waiting for transfers between devices: 135 us -> none  [the longest x1 126 us: local(): lax.all_gather(out_weight, 'seq', axis=0, tiled=True)]
    all_to_all x4 -> x0, waiting for transfers between devices: 51.5 us -> none  [the longest x1 17.6 us: to_positions(): lax.all_to_all(query_rows.reshape(frames, group_size, 1, row_width), 'seq...]
    all_to_all x4 -> x0, starting transfers between devices: 23.1 us -> none  [the longest x1 8.31 us: to_positions(): lax.all_to_all(query_rows.reshape(frames, group_size, 1, row_width), 'seq...]
    dot_general x5 -> x0, matrix products: 16.8 us -> none  [the longest x1 7.66 us: local(): jnp.dot(head_columns, lax.all_gather(out_weight, 'seq', axis=0, tiled=Tru...]
    gather x5 -> x0, local copies, waits for them, and re-layouts: 10 us -> none  [the longest x1 4.19 us: local(): queries[order_map]]
    another operation x5 -> x0, local copies, waits for them, and re-layouts: 5.54 us -> none  [the longest x3 3.71 us: split_heads(): array.reshape(array.shape[0], head_count, array.shape[1] // head_count)]
    sub x2 -> x0, other arithmetic: 4.6 us -> none  [attend_rows(): weights = jnp.where(visible, jnp.exp(scores - row_max), 0.0)]
  transfers between devices with their start and end apart: 6 -> 0, of which waited for: 6 -> 0; matrix products, arithmetic and copies ran while one was open for 8% -> 0% of each run, Pallas kernels for 0% -> 0%
where the time goes in v1:
time: 151 us; the launch traced here: 150 us
  Pallas kernels  143 us (95%)
  local copies, waits for them, and re-layouts  7.49 us (5%)
    pallas_call x1, Pallas kernels, branch_call(): pl.pallas_call(functools.partial(branch_kernel, frames, slots, depth), ou...  143 us
    unnamed x19, local copies, waits for them, and re-layouts  7.31 us

profile of v1, /device:TPU:0, one launch (start us, length us, event | category | flops | bytes accessed | tf_op | source)
XLA Modules:
  0.0 150.1 jit_solution(1183708840354327289)
XLA Ops:
  0.0 0.0 copy-start
  0.0 0.0 copy-start.7
  0.0 0.7 copy-done.7
  0.7 0.0 copy-start.6
  0.7 0.1 copy.9
  0.8 0.6 copy-done.6
  1.4 0.0 copy-done
  1.4 0.1 broadcast_bitcast_fusion
  1.5 0.0 copy-start.5
  1.5 0.1 broadcast_in_dim.22.bias_ref
  1.6 0.6 copy-done.5
  2.2 0.0 copy-start.1
  2.2 1.1 copy-done.1
  3.3 0.0 copy-start.2
  3.3 1.1 copy-done.2
  4.4 0.0 copy-start.3
  4.4 1.1 copy-done.3
  5.6 0.0 copy-start.4
  5.6 1.1 copy-done.4
  6.6 142.6 %branch_12.1 = bf16[256,1536]{1,0:T(8,128)(2,1)S(1)} custom-call(s32[12]{0:T(128)S(1)} %iota.3.heads_ref, s32[1,1536]{1,0:T(1,128)S(1)} %bitcast.8, f32[12,4,128]{2,1,0:T(4,128)S(1)} %broadcast_in_dim.22.bias_ref, s32[1,256]{1,0:T(1,128)S(1)} %bitcast.9, bf16[256,1536]{1,0:T(8,128)(2,1)S(1)} %copy-done.1, bf16[256,1536]{1,0:T(8,128)(2,1)S(1)} %copy-done.2, ...), custom_call_target="tpu_custom_call" | custom-call | tf_op jit(solution)/shard_map/branch_12/pallas_call | solution.py:395
  149.3 0.9 copy.14
  (4 shorter events, 0.0 us)
Async XLA Ops:
  0.0 1.4 copy-start
  0.0 0.7 copy-start.7
  0.7 0.7 copy-start.6
  1.5 0.7 copy-start.5
  2.2 1.1 copy-start.1
  3.3 1.1 copy-start.2
  4.4 1.1 copy-start.3
  5.6 1.1 copy-start.4
